TPU v7x, 512 devices: a whole 4x8x8 slice. The times are simulated.
512 devices in a mesh: seq: 128 (over z_lo, x, y), dp: 4 (over z_hi, core).
Axes of the slice: x: 4, y: 8, z: 8 (z_hi: 2, z_lo: 4; z = z_hi * 4 + z_lo), core: 2. Of those that a mesh axis runs over, the one named last changes fastest.
Arguments:
- byte_qkv: bfloat16 [4, 32768, 3072], P('dp', 'seq'), may hold values from -6 to 6
- patch_qkv: bfloat16 [4, 8192, 3072], P('dp', 'seq'), may hold values from -6 to 6
- patch_gain: float32 [3072], replicated, may hold values from 0.3 to 1.5
- out_grad: bfloat16 [4, 32768, 1024], P('dp', 'seq'), may hold values from -48 to 48
- patch_slot: int32 [4, 32768], P('dp', 'seq'), may hold values from 0 to 63, as said below
- lead: int32 [4, 128], P('dp', 'seq'), may hold values from 0 to 15, as said below
Outputs:
- byte_grad: bfloat16 [4, 32768, 3072], P('dp', 'seq')
- patch_grad: bfloat16 [4, 8192, 3072], P('dp', 'seq')
- gain_grad: float32 [3072], replicated
Inputs may be any that keep to these rules, and one draw needn't show every extreme that they name: Patches are runs of 1 to 31 bytes of a stream. A patch is owned by the device that holds its first byte; each device numbers the patches starting on it 0, 1, 2 and so on in order, and patch_slot gives each byte the number of its patch on the owning device. Every device holds the first byte of at least one patch. lead[s, d] bytes at the start of device d's run of stream s belong to the last patch that starts on device d - 1; lead[s, 0] = 0.
All inputs are finite; a program needn't handle non-finite values.
Results may differ from a plain program's by a relative error of at most 0.011.
Values may be sent and summed in bfloat16 or wider, within the bound.
A program may use at most 128 MiB of HBM per device.

v0:
```python
import math
import jax
import jax.numpy as jnp
from jax import lax
from jax.sharding import PartitionSpec as P

HEADS = 8
HEAD_DIM = 128
WIN = 512


def shifted(value, axis, steps):
    count = lax.axis_size(axis)
    initial, last = (max(0, -steps), min(count, count - steps))
    return lax.ppermute(value, axis, [(source, source + steps) for source in range(initial, last)])


def local(byte_qkv, patch_qkv, patch_gain, out_grad, patch_slot, lead):
    own_bytes = byte_qkv[0]
    patch_table = patch_qkv[0]
    cotangent = out_grad[0]
    slot_ids = patch_slot[0]
    row_count = own_bytes.shape[0]
    feature_count = cotangent.shape[1]
    capacity = patch_table.shape[0]
    first_pos = lax.axis_index("seq") * row_count
    reach_blocks = -(-WIN // row_count)
    inv_sqrt = 1.0 / math.sqrt(HEAD_DIM)
    local_rows = lax.broadcasted_iota(jnp.int32, (row_count,), 0)
    leading = local_rows < lead[0, 0]
    owned_slots = jnp.where(leading, -1, slot_ids)
    last_slot = jnp.max(owned_slots)
    last_row = lax.dynamic_slice_in_dim(patch_table, last_slot, 1, 0)
    prev_row = shifted(last_row, "seq", 1)
    slot_axis = lax.broadcasted_iota(jnp.int32, (row_count, capacity), 1)
    pick_rows = (slot_ids[:, None] == slot_axis).astype(jnp.bfloat16)
    patch_rows = jnp.dot(pick_rows, patch_table, preferred_element_type=jnp.float32)
    patch_rows = jnp.where(leading[:, None], prev_row.astype(jnp.float32), patch_rows)
    hidden = (patch_gain * patch_rows + own_bytes.astype(jnp.float32)).astype(jnp.bfloat16)
    queries = hidden[:, :feature_count]
    key_values = hidden[:, feature_count:]
    blocks = [key_values]
    arrived = shifted(key_values, "seq", 1)
    blocks.append(arrived)
    steps_back = 2
    arrived = shifted(key_values, "seq", steps_back)
    blocks.append(arrived)
    window = jnp.concatenate(blocks[::-1], axis=0)
    key_count = window.shape[0]
    query_pos = first_pos + local_rows
    key_pos = (
        first_pos - reach_blocks * row_count + lax.broadcasted_iota(jnp.int32, (key_count,), 0)
    )
    in_window = (
        (key_pos[None, :] <= query_pos[:, None])
        & (key_pos[None, :] > query_pos[:, None] - WIN)
        & (key_pos[None, :] >= 0)
    )
    query_parts = []
    key_parts = []
    value_parts = []
    max_list = []
    total_list = []
    delta_list = []
    for head_index in range(HEADS):
        low = head_index * HEAD_DIM
        query_head = queries[:, low : low + HEAD_DIM]
        cot_head = cotangent[:, low : low + HEAD_DIM]
        key_head = window[:, low : low + HEAD_DIM]
        value_head = window[:, feature_count + low : feature_count + low + HEAD_DIM]
        scores = (
            jnp.einsum("qe,ke->qk", query_head, key_head, preferred_element_type=jnp.float32)
            * inv_sqrt
        )
        scores = jnp.where(in_window, scores, -jnp.inf)
        row_max = jnp.max(scores, axis=1, keepdims=True)
        exponent = jnp.where(in_window, jnp.exp(scores - row_max), 0.0)
        row_total = jnp.sum(exponent, axis=1, keepdims=True)
        attn_prob = exponent / row_total
        prob_half = attn_prob.astype(jnp.bfloat16)
        value_parts.append(
            jnp.einsum("qk,qe->ke", prob_half, cot_head, preferred_element_type=jnp.float32)
        )
        prob_grad = jnp.einsum(
            "qe,ke->qk", cot_head, value_head, preferred_element_type=jnp.float32
        )
        row_delta = jnp.sum(attn_prob * prob_grad, axis=1, keepdims=True)
        score_grad = (attn_prob * (prob_grad - row_delta)).astype(jnp.bfloat16)
        query_parts.append(
            jnp.einsum("qk,ke->qe", score_grad, key_head, preferred_element_type=jnp.float32)
            * inv_sqrt
        )
        key_parts.append(
            jnp.einsum("qk,qe->ke", score_grad, query_head, preferred_element_type=jnp.float32)
            * inv_sqrt
        )
        max_list.append(row_max[:, 0])
        total_list.append(row_total[:, 0])
        delta_list.append(row_delta[:, 0])
    query_grad = jnp.concatenate(query_parts, axis=1)
    key_part = jnp.concatenate(key_parts, axis=1)
    value_part = jnp.concatenate(value_parts, axis=1)
    back_grads = jnp.concatenate([key_part, value_part], axis=1)
    own_grads = back_grads[key_count - row_count :]
    for steps_back in range(1, reach_blocks + 1):
        piece_first = (reach_blocks - steps_back) * row_count
        piece = back_grads[piece_first : piece_first + row_count]
        own_grads = own_grads + shifted(piece, "seq", -steps_back)
    hidden_grad = jnp.concatenate([query_grad, own_grads], axis=1)
    byte_grad = hidden_grad.astype(jnp.bfloat16)[None]
    lead_sum = jnp.sum(jnp.where(leading[:, None], hidden_grad, 0.0), axis=0, keepdims=True)
    from_next = shifted(lead_sum, "seq", -1)
    slot_column = lax.broadcasted_iota(jnp.int32, (capacity, row_count), 0)
    member = ((slot_ids[None, :] == slot_column) & jnp.logical_not(leading)[None, :]).astype(
        jnp.float32
    )
    slot_sums = jnp.dot(
        member, hidden_grad, precision=lax.Precision.HIGHEST, preferred_element_type=jnp.float32
    )
    slot_index = lax.broadcasted_iota(jnp.int32, (capacity, 1), 0)
    slot_sums = slot_sums + (slot_index == last_slot).astype(jnp.float32) * from_next
    patch_grad = (patch_gain * slot_sums).astype(jnp.bfloat16)[None]
    gain_term = jnp.sum(slot_sums * patch_table.astype(jnp.float32), axis=0)
    gain_grad = lax.psum(gain_term, ("seq", "dp")) / row_count
    return (byte_grad, patch_grad, gain_grad)


def solution(mesh):
    placed = (
        P("dp", "seq", None),
        P("dp", "seq", None),
        P(),
        P("dp", "seq", None),
        P("dp", "seq"),
        P("dp", "seq"),
    )
    return jax.shard_map(
        local,
        mesh=mesh,
        in_specs=placed,
        out_specs=(P("dp", "seq", None), P("dp", "seq", None), P()),
        check_vma=False,
    )
```

profile of v0, /device:TPU:1, one launch (start us, length us, event | category | flops | bytes accessed | tf_op | source)
XLA Modules:
  0.0 348.9 jit_solution(16617319942461404328)
XLA Ops:
  1.3 1.3 select_reduce_fusion.1
  4.5 0.8 dynamic-slice_bitcast_fusion
  5.4 4.0 %collective-permute-start = (bf16[1,3072]{1,0:T(2,128)(2,1)S(1)}, bf16[1,3072]{1,0:T(2,128)(2,1)S(1)}, u32[]{:S(2)}, u32[]{:S(2)}) collective-permute-start(bf16[1,3072]{1,0:T(2,128)(2,1)S(1)} %dynamic-slice_bitcast_fusion), channel_id=1, source_target_pairs={{0,4},{4,8},{8,12},{12,16},{16,20},{20,24},{24,28},{28,32},{32,36}... | collective-permute-start | bytes 18440 | tf_op jit(solution)/shard_map/ppermute | solution.py:15
  10.2 2.3 fusion
  12.6 4.6 %collective-permute-start.2 = (bf16[256,2048]{1,0:T(8,128)(2,1)S(1)}, bf16[256,2048]{1,0:T(8,128)(2,1)}, u32[]{:S(2)}, u32[]{:S(2)}) collective-permute-start(bf16[256,2048]{1,0:T(8,128)(2,1)S(1)} %slice.154), channel_id=1, source_target_pairs={{0,4},{4,8},{8,12},{12,16},{16,20},{20,24},{24,28},{28,32},{32,36}... | collective-permute-start | bytes 3145736 | tf_op jit(solution)/shard_map/ppermute | solution.py:15
  17.2 5.1 %collective-permute-start.1 = (bf16[256,2048]{1,0:T(8,128)(2,1)S(1)}, bf16[256,2048]{1,0:T(8,128)(2,1)}, u32[]{:S(2)}, u32[]{:S(2)}) collective-permute-start(bf16[256,2048]{1,0:T(8,128)(2,1)S(1)} %slice.154), channel_id=1, source_target_pairs={{0,8},{4,12},{8,16},{12,20},{16,24},{20,28},{24,32},{28,36},{32,40... | collective-permute-start | bytes 3145736 | tf_op jit(solution)/shard_map/ppermute | solution.py:15
  23.0 10.7 %collective-permute-done.2 = bf16[256,2048]{1,0:T(8,128)(2,1)} collective-permute-done((bf16[256,2048]{1,0:T(8,128)(2,1)S(1)}, bf16[256,2048]{1,0:T(8,128)(2,1)}, u32[]{:S(2)}, u32[]{:S(2)}) %collective-permute-start.2) | collective-permute-done | bytes 1048608 | tf_op jit(solution)/shard_map/ppermute | solution.py:15
  33.6 24.7 %collective-permute-done.1 = bf16[256,2048]{1,0:T(8,128)(2,1)} collective-permute-done((bf16[256,2048]{1,0:T(8,128)(2,1)S(1)}, bf16[256,2048]{1,0:T(8,128)(2,1)}, u32[]{:S(2)}, u32[]{:S(2)}) %collective-permute-start.1) | collective-permute-done | bytes 1048608 | tf_op jit(solution)/shard_map/ppermute | solution.py:15
  58.3 1.8 pad_maximum_fusion
  64.9 0.9 fusion.33
  65.8 1.4 multiply_reduce_fusion.1
  67.2 1.1 multiply_reduce_fusion.3
  68.3 1.1 multiply_reduce_fusion.2
  69.4 1.0 multiply_convert_fusion.6
  71.9 1.0 multiply_convert_fusion.1
  72.9 1.2 multiply_convert_fusion.3
  81.1 1.3 collective-permute-start.4
  82.4 1.3 collective-permute-start.3
  85.6 29.1 %collective-permute-done.4 = f32[256,2048]{1,0:T(8,128)S(1)} collective-permute-done((f32[256,2048]{1,0:T(8,128)S(1)}, f32[256,2048]{1,0:T(8,128)S(1)}, u32[]{:S(2)}, u32[]{:S(2)}) %collective-permute-start.4) | collective-permute-done | bytes 2097184 | tf_op jit(solution)/shard_map/ppermute | solution.py:15
  114.7 46.9 %collective-permute-done.3 = f32[256,2048]{1,0:T(8,128)S(1)} collective-permute-done((f32[256,2048]{1,0:T(8,128)S(1)}, f32[256,2048]{1,0:T(8,128)S(1)}, u32[]{:S(2)}, u32[]{:S(2)}) %collective-permute-start.3) | collective-permute-done | bytes 2097184 | tf_op jit(solution)/shard_map/ppermute | solution.py:15
  162.7 1.3 collective-permute-start.5
  164.5 44.3 %collective-permute-done.5 = f32[1,3072]{1,0:T(1,128)S(1)} collective-permute-done((f32[1,3072]{1,0:T(1,128)S(1)}, f32[1,3072]{1,0:T(1,128)S(1)}, u32[]{:S(2)}, u32[]{:S(2)}) %collective-permute-start.5) | collective-permute-done | bytes 12320 | tf_op jit(solution)/shard_map/ppermute | solution.py:15
  208.9 2.2 multiply_reduce_fusion
  211.1 137.2 %psum.7 = f32[3072]{0:T(1024)S(1)} all-reduce(f32[3072]{0:T(1024)S(1)} %get-tuple-element.20), channel_id=1, replica_groups=mesh['seq'=128,'dp'=4] {'seq','dp'}, use_global_device_ids=true, to_apply=%region_27.28 | all-reduce | flops 3072 | bytes 24576 | tf_op jit(solution)/shard_map/psum | solution.py:124
  (68 shorter events, 18.6 us)
Async XLA Ops:
  5.4 4.9 %collective-permute-start = (bf16[1,3072]{1,0:T(2,128)(2,1)S(1)}, bf16[1,3072]{1,0:T(2,128)(2,1)S(1)}, u32[]{:S(2)}, u32[]{:S(2)}) collective-permute-start(bf16[1,3072]{1,0:T(2,128)(2,1)S(1)} %dynamic-slice_bitcast_fusion), channel_id=1, source_target_pairs={{0,4},{4,8},{8,12},{12,16},{16,20},{20,24},{24,28},{28,32},{32,36}... | collective-permute-start | bytes 18440 | tf_op jit(solution)/shard_map/ppermute | solution.py:15
  12.6 21.1 %collective-permute-start.2 = (bf16[256,2048]{1,0:T(8,128)(2,1)S(1)}, bf16[256,2048]{1,0:T(8,128)(2,1)}, u32[]{:S(2)}, u32[]{:S(2)}) collective-permute-start(bf16[256,2048]{1,0:T(8,128)(2,1)S(1)} %slice.154), channel_id=1, source_target_pairs={{0,4},{4,8},{8,12},{12,16},{16,20},{20,24},{24,28},{28,32},{32,36}... | collective-permute-start | bytes 3145736 | tf_op jit(solution)/shard_map/ppermute | solution.py:15
  17.2 41.1 %collective-permute-start.1 = (bf16[256,2048]{1,0:T(8,128)(2,1)S(1)}, bf16[256,2048]{1,0:T(8,128)(2,1)}, u32[]{:S(2)}, u32[]{:S(2)}) collective-permute-start(bf16[256,2048]{1,0:T(8,128)(2,1)S(1)} %slice.154), channel_id=1, source_target_pairs={{0,8},{4,12},{8,16},{12,20},{16,24},{20,28},{24,32},{28,36},{32,40... | collective-permute-start | bytes 3145736 | tf_op jit(solution)/shard_map/ppermute | solution.py:15
  62.0 1.8 copy-start.1
  81.1 33.7 %collective-permute-start.4 = (f32[256,2048]{1,0:T(8,128)S(1)}, f32[256,2048]{1,0:T(8,128)S(1)}, u32[]{:S(2)}, u32[]{:S(2)}) collective-permute-start(f32[256,2048]{1,0:T(8,128)S(1)} %get-tuple-element.19), channel_id=1, source_target_pairs={{8,0},{12,4},{16,8},{20,12},{24,16},{28,20},{32,24},{36,28},{40,32... | collective-permute-start | bytes 6291464 | tf_op jit(solution)/shard_map/ppermute | solution.py:15
  82.4 79.3 %collective-permute-start.3 = (f32[256,2048]{1,0:T(8,128)S(1)}, f32[256,2048]{1,0:T(8,128)S(1)}, u32[]{:S(2)}, u32[]{:S(2)}) collective-permute-start(f32[256,2048]{1,0:T(8,128)S(1)} %get-tuple-element.18), channel_id=1, source_target_pairs={{4,0},{8,4},{12,8},{16,12},{20,16},{24,20},{28,24},{32,28},{36,32}... | collective-permute-start | bytes 6291464 | tf_op jit(solution)/shard_map/ppermute | solution.py:15
  162.7 46.1 %collective-permute-start.5 = (f32[1,3072]{1,0:T(1,128)S(1)}, f32[1,3072]{1,0:T(1,128)S(1)}, u32[]{:S(2)}, u32[]{:S(2)}) collective-permute-start(f32[1,3072]{1,0:T(1,128)S(1)} %bitcast.89), channel_id=1, source_target_pairs={{4,0},{8,4},{12,8},{16,12},{20,16},{24,20},{28,24},{32,28},{36,32}... | collective-permute-start | bytes 36872 | tf_op jit(solution)/shard_map/ppermute | solution.py:15
  164.0 44.8 %copy-start = (bf16[1,64,3072]{2,1,0:T(8,128)(2,1)S(1)}, bf16[1,64,3072]{2,1,0:T(8,128)(2,1)}, u32[]{:S(2)}) copy-start(bf16[1,64,3072]{2,1,0:T(8,128)(2,1)} %param.7) | copy-start | bytes 1179652
  164.1 44.8 %copy-start.2 = (f32[3072]{0:T(1024)S(1)}, f32[3072]{0:T(1024)}, u32[]{:S(2)}) copy-start(f32[3072]{0:T(1024)} %param.8) | copy-start | bytes 36868
  164.1 44.8 %copy-start.3 = (s32[1,256]{1,0:T(1,128)S(1)}, s32[1,256]{1,0:T(1,128)}, u32[]{:S(2)}) copy-start(s32[1,256]{1,0:T(1,128)} %param.10) | copy-start | bytes 3076
  164.5 46.6 %copy-start.4 = (bf16[1,256,3072]{2,1,0:T(8,128)(2,1)}, bf16[1,256,3072]{2,1,0:T(8,128)(2,1)S(1)}, u32[]{:S(2)}) copy-start(bf16[1,256,3072]{2,1,0:T(8,128)(2,1)S(1)} %bitcast_dynamic-update-slice_fusion) | copy-start | bytes 4718596
where the time goes:
time: 349 us
  waiting for transfers between devices  157 us (45%)
  blocking collectives  137 us (39%)
  matrix products  23.3 us (7%)
  starting transfers between devices  17.6 us (5%)
  other arithmetic  9.05 us (3%)
  between operations  3.69 us (1%)
    ppermute x6, waiting for transfers between devices, shifted(): lax.ppermute(value, axis, [(source, source + steps) for source in range(i...  157 us
    psum x1, blocking collectives, local(): gain_grad = lax.psum(gain_term, ('seq', 'dp')) / row_count  137 us
    ppermute x6, starting transfers between devices, shifted(): lax.ppermute(value, axis, [(source, source + steps) for source in range(i...  17.6 us
  transfers between devices with their start and end apart: 6, of which 6 were waited for; matrix products, arithmetic and copies ran while one was open for 1% of the time, Pallas kernels for 0%

commit v1 on v0

--- a/solution.py
+++ b/solution.py
@@ -121,7 +121,7 @@
     slot_sums = slot_sums + (slot_index == last_slot).astype(jnp.float32) * from_next
     patch_grad = (patch_gain * slot_sums).astype(jnp.bfloat16)[None]
     gain_term = jnp.sum(slot_sums * patch_table.astype(jnp.float32), axis=0)
-    gain_grad = lax.psum(gain_term, ("seq", "dp")) / row_count
+    gain_grad = lax.psum(lax.psum(gain_term, "seq"), "dp") / row_count
     return (byte_grad, patch_grad, gain_grad)
 
 

time: 349 us -> 985 us (2.82)
  blocking collectives: 137 us -> 774 us
    psum x1 -> x2, blocking collectives: 137 us -> 774 us  [local(): gain_grad = lax.psum(lax.psum(gain_term, 'seq'), 'dp') / row_count]
  transfers between devices with their start and end apart: 6 -> 6, of which waited for: 6 -> 6; matrix products, arithmetic and copies ran while one was open for 1% -> 0% of each run, Pallas kernels for 0% -> 0%
where the time goes in v1:
time: 985 us
  blocking collectives  774 us (79%)
  waiting for transfers between devices  157 us (16%)
  matrix products  23.1 us (2%)
  starting transfers between devices  17.6 us (2%)
    psum x2, blocking collectives, local(): gain_grad = lax.psum(lax.psum(gain_term, 'seq'), 'dp') / row_count  774 us
    ppermute x6, waiting for transfers between devices, shifted(): lax.ppermute(value, axis, [(source, source + steps) for source in range(i...  157 us
  transfers between devices with their start and end apart: 6, of which 6 were waited for; matrix products, arithmetic and copies ran while one was open for 0% of the time, Pallas kernels for 0%

profile of v1, /device:TPU:1, one launch (start us, length us, event | category | flops | bytes accessed | tf_op | source)
XLA Modules:
  0.0 985.0 jit_solution(18088696107435730698)
XLA Ops:
  1.3 1.3 select_reduce_fusion.1
  5.4 4.0 collective-permute-start
  10.2 2.3 fusion
  12.6 4.6 collective-permute-start.2
  17.2 5.1 collective-permute-start.1
  23.0 10.7 %collective-permute-done.2 = bf16[256,2048]{1,0:T(8,128)(2,1)} collective-permute-done((bf16[256,2048]{1,0:T(8,128)(2,1)S(1)}, bf16[256,2048]{1,0:T(8,128)(2,1)}, u32[]{:S(2)}, u32[]{:S(2)}) %collective-permute-start.2) | collective-permute-done | bytes 1048608 | tf_op jit(solution)/shard_map/ppermute | solution.py:15
  33.6 24.7 %collective-permute-done.1 = bf16[256,2048]{1,0:T(8,128)(2,1)} collective-permute-done((bf16[256,2048]{1,0:T(8,128)(2,1)S(1)}, bf16[256,2048]{1,0:T(8,128)(2,1)}, u32[]{:S(2)}, u32[]{:S(2)}) %collective-permute-start.1) | collective-permute-done | bytes 1048608 | tf_op jit(solution)/shard_map/ppermute | solution.py:15
  58.3 1.7 pad_maximum_fusion
  64.8 0.9 fusion.33
  65.7 1.4 multiply_reduce_fusion.1
  67.1 1.0 multiply_reduce_fusion.3
  68.1 1.0 multiply_reduce_fusion.2
  69.1 1.0 multiply_convert_fusion.6
  71.6 0.9 multiply_convert_fusion.1
  72.6 1.2 multiply_convert_fusion.3
  80.7 1.3 collective-permute-start.4
  82.0 1.3 collective-permute-start.3
  85.2 29.1 %collective-permute-done.4 = f32[256,2048]{1,0:T(8,128)S(1)} collective-permute-done((f32[256,2048]{1,0:T(8,128)S(1)}, f32[256,2048]{1,0:T(8,128)S(1)}, u32[]{:S(2)}, u32[]{:S(2)}) %collective-permute-start.4) | collective-permute-done | bytes 2097184 | tf_op jit(solution)/shard_map/ppermute | solution.py:15
  114.4 46.9 %collective-permute-done.3 = f32[256,2048]{1,0:T(8,128)S(1)} collective-permute-done((f32[256,2048]{1,0:T(8,128)S(1)}, f32[256,2048]{1,0:T(8,128)S(1)}, u32[]{:S(2)}, u32[]{:S(2)}) %collective-permute-start.3) | collective-permute-done | bytes 2097184 | tf_op jit(solution)/shard_map/ppermute | solution.py:15
  162.3 1.3 collective-permute-start.5
  164.1 44.3 %collective-permute-done.5 = f32[1,3072]{1,0:T(1,128)S(1)} collective-permute-done((f32[1,3072]{1,0:T(1,128)S(1)}, f32[1,3072]{1,0:T(1,128)S(1)}, u32[]{:S(2)}, u32[]{:S(2)}) %collective-permute-start.5) | collective-permute-done | bytes 12320 | tf_op jit(solution)/shard_map/ppermute | solution.py:15
  208.5 2.2 multiply_reduce_fusion
  210.7 643.2 %psum.14 = f32[3072]{0:T(1024)S(1)} all-reduce(f32[3072]{0:T(1024)S(1)} %get-tuple-element.20), channel_id=1, replica_groups=mesh['seq'=128,'dp'=4] {'seq'}, use_global_device_ids=true, to_apply=%region_27.28 | all-reduce | flops 3072 | bytes 24576 | tf_op jit(solution)/shard_map/psum | solution.py:124
  853.8 130.5 %psum.15 = f32[3072]{0:T(1024)S(1)} all-reduce(f32[3072]{0:T(1024)S(1)} %psum.14), channel_id=1, replica_groups=mesh['seq'=128,'dp'=4] {'dp'}, use_global_device_ids=true, to_apply=%region_28.29 | all-reduce | flops 3072 | bytes 24576 | tf_op jit(solution)/shard_map/psum | solution.py:124
  (69 shorter events, 19.4 us)
Async XLA Ops:
  5.4 4.9 collective-permute-start
  12.6 21.1 %collective-permute-start.2 = (bf16[256,2048]{1,0:T(8,128)(2,1)S(1)}, bf16[256,2048]{1,0:T(8,128)(2,1)}, u32[]{:S(2)}, u32[]{:S(2)}) collective-permute-start(bf16[256,2048]{1,0:T(8,128)(2,1)S(1)} %slice.154), channel_id=1, source_target_pairs={{0,4},{4,8},{8,12},{12,16},{16,20},{20,24},{24,28},{28,32},{32,36}... | collective-permute-start | bytes 3145736 | tf_op jit(solution)/shard_map/ppermute | solution.py:15
  17.2 41.1 %collective-permute-start.1 = (bf16[256,2048]{1,0:T(8,128)(2,1)S(1)}, bf16[256,2048]{1,0:T(8,128)(2,1)}, u32[]{:S(2)}, u32[]{:S(2)}) collective-permute-start(bf16[256,2048]{1,0:T(8,128)(2,1)S(1)} %slice.154), channel_id=1, source_target_pairs={{0,8},{4,12},{8,16},{12,20},{16,24},{20,28},{24,32},{28,36},{32,40... | collective-permute-start | bytes 3145736 | tf_op jit(solution)/shard_map/ppermute | solution.py:15
  61.9 1.8 copy-start.1
  80.7 33.7 %collective-permute-start.4 = (f32[256,2048]{1,0:T(8,128)S(1)}, f32[256,2048]{1,0:T(8,128)S(1)}, u32[]{:S(2)}, u32[]{:S(2)}) collective-permute-start(f32[256,2048]{1,0:T(8,128)S(1)} %get-tuple-element.19), channel_id=1, source_target_pairs={{8,0},{12,4},{16,8},{20,12},{24,16},{28,20},{32,24},{36,28},{40,32... | collective-permute-start | bytes 6291464 | tf_op jit(solution)/shard_map/ppermute | solution.py:15
  82.0 79.3 %collective-permute-start.3 = (f32[256,2048]{1,0:T(8,128)S(1)}, f32[256,2048]{1,0:T(8,128)S(1)}, u32[]{:S(2)}, u32[]{:S(2)}) collective-permute-start(f32[256,2048]{1,0:T(8,128)S(1)} %get-tuple-element.18), channel_id=1, source_target_pairs={{4,0},{8,4},{12,8},{16,12},{20,16},{24,20},{28,24},{32,28},{36,32}... | collective-permute-start | bytes 6291464 | tf_op jit(solution)/shard_map/ppermute | solution.py:15
  162.3 46.1 %collective-permute-start.5 = (f32[1,3072]{1,0:T(1,128)S(1)}, f32[1,3072]{1,0:T(1,128)S(1)}, u32[]{:S(2)}, u32[]{:S(2)}) collective-permute-start(f32[1,3072]{1,0:T(1,128)S(1)} %bitcast.89), channel_id=1, source_target_pairs={{4,0},{8,4},{12,8},{16,12},{20,16},{24,20},{28,24},{32,28},{36,32}... | collective-permute-start | bytes 36872 | tf_op jit(solution)/shard_map/ppermute | solution.py:15
  163.6 44.8 %copy-start = (bf16[1,64,3072]{2,1,0:T(8,128)(2,1)S(1)}, bf16[1,64,3072]{2,1,0:T(8,128)(2,1)}, u32[]{:S(2)}) copy-start(bf16[1,64,3072]{2,1,0:T(8,128)(2,1)} %param.7) | copy-start | bytes 1179652
  163.7 44.8 %copy-start.2 = (f32[3072]{0:T(1024)S(1)}, f32[3072]{0:T(1024)}, u32[]{:S(2)}) copy-start(f32[3072]{0:T(1024)} %param.8) | copy-start | bytes 36868
  163.7 44.8 %copy-start.3 = (s32[1,256]{1,0:T(1,128)S(1)}, s32[1,256]{1,0:T(1,128)}, u32[]{:S(2)}) copy-start(s32[1,256]{1,0:T(1,128)} %param.10) | copy-start | bytes 3076
  164.1 46.6 %copy-start.4 = (bf16[1,256,3072]{2,1,0:T(8,128)(2,1)}, bf16[1,256,3072]{2,1,0:T(8,128)(2,1)S(1)}, u32[]{:S(2)}) copy-start(bf16[1,256,3072]{2,1,0:T(8,128)(2,1)S(1)} %bitcast_dynamic-update-slice_fusion) | copy-start | bytes 4718596
